TPU v7x, 32 devices: a whole 2x2x4 slice. The times are simulated.
32 devices in a mesh: groups: 2 (over y), view: 16 (over z, x, core).
Axes of the slice: x: 2, y: 2, z: 4, core: 2. Of those that a mesh axis runs over, the one named last changes fastest.
Arguments:
- embeddings: bfloat16 [32, 1024, 768], P(('groups', 'view')), parts along dimension 0, may hold values from -6 to 6
- projection: bfloat16 [768, 768], replicated, may hold values from -0.21875 to 0.21875
- owners: int32 [32, 128, 1], P(('groups', 'view')), parts along dimension 0, may hold values from 0 to 15; in each aligned block of 128 rows (0 to 127, 128 to 255, ..., all dimensions but the last counted through in order) at most 16 rows name the same one
- local_blocks: int32 [32, 128], P(('groups', 'view')), parts along dimension 0, may hold values from 0 to 63
- patches: int32 [32, 4, 2048], P(('groups', 'view')), parts along dimension 0, may hold values from 0 to 1023
- weights: float32 [32, 4, 2048], P(('groups', 'view')), parts along dimension 0, may hold values from 0.05 to 1
Outputs:
- targets: bfloat16 [32768, 768], P(('groups', 'view')), parts along dimension 0
There are 2 independent parts, one for each index of `groups`. A program takes and returns all parts, laid end to end along the dimension named above; an argument that names none is the same for every part. Nothing has to cross between parts.
Inputs may be any that keep to these rules, and one draw needn't show every extreme that they name: `owners`: among the 128 slots of one view, at most 16 name one owner; this is reached.
All inputs are finite; a program needn't handle non-finite values.
Results may differ from a plain program's by a relative error of at most 0.014.
Values may be sent and summed in bfloat16 or wider, within the bound.
A program may use at most 64 MiB of HBM per device.

v0:
```python
import jax
import jax.numpy as jnp
from jax import lax
from jax.sharding import PartitionSpec as P

BLK_DEV = 64


def per_device(embeddings, projection, owners, local_blocks, patches, weights):
    nview = lax.axis_size("view")
    slots = owners.shape[1]
    width = embeddings.shape[2]
    npatch = embeddings.shape[1]
    points = patches.shape[2] // slots
    blk_count = BLK_DEV
    cap_slots = max(2, 2 * slots // nview)
    table = embeddings[0]
    index = patches[0]
    wts = weights[0]
    patch_ids = jnp.arange(npatch, dtype=jnp.int32)
    selection = jnp.zeros((slots * points, npatch), jnp.float32)
    for k in range(4):
        selection = selection + jnp.where(
            index[k][:, None] == patch_ids[None, :], wts[k][:, None], 0.0
        )
    w_high = selection.astype(jnp.bfloat16)
    w_low = (selection - w_high.astype(jnp.float32)).astype(jnp.bfloat16)
    blended = jnp.dot(w_high, table, preferred_element_type=jnp.float32) + jnp.dot(
        w_low, table, preferred_element_type=jnp.float32
    )
    blended = blended.astype(jnp.bfloat16)
    point_wts = jnp.sum(wts, axis=0).reshape(slots, points)
    target_dev = owners[0, :, 0]
    slot_ids = jnp.arange(slots, dtype=jnp.int32)
    same_owner = target_dev[:, None] == target_dev[None, :]
    earlier = slot_ids[None, :] < slot_ids[:, None]
    rank = jnp.sum((same_owner & earlier).astype(jnp.int32), axis=1)
    position = target_dev * cap_slots + rank
    total_slots = nview * cap_slots
    placing = jnp.arange(total_slots, dtype=jnp.int32)[:, None] == position[None, :]
    send_rows = jnp.dot(
        placing.astype(jnp.bfloat16),
        blended.reshape(slots, points * width),
        preferred_element_type=jnp.float32,
    ).astype(jnp.bfloat16)
    send_wts = jnp.dot(placing.astype(jnp.float32), point_wts, precision=lax.Precision.HIGHEST)
    send_ids = jnp.sum(placing.astype(jnp.int32) * local_blocks[0][None, :], axis=1)
    send_rows = send_rows.reshape(nview, cap_slots, points, width)
    send_wts = send_wts.reshape(nview, cap_slots, points)
    send_ids = send_ids.reshape(nview, cap_slots)
    rows_in = lax.all_to_all(send_rows, "view", split_axis=0, concat_axis=0, tiled=True)
    wts_in = lax.all_to_all(
        send_wts.astype(jnp.bfloat16), "view", split_axis=0, concat_axis=0, tiled=True
    ).astype(send_wts.dtype)
    ids_in = lax.all_to_all(send_ids, "view", split_axis=0, concat_axis=0, tiled=True)
    projected = jnp.einsum(
        "ncsd,de->ncse", rows_in, projection, preferred_element_type=jnp.float32
    ).astype(jnp.bfloat16)
    flat_rows = projected.reshape(total_slots, points * width)
    flat_wts = wts_in.reshape(total_slots, points)
    flat_ids = ids_in.reshape(total_slots)
    selector = jnp.arange(blk_count, dtype=jnp.int32)[:, None] == flat_ids[None, :]
    sums = jnp.dot(selector.astype(jnp.bfloat16), flat_rows, preferred_element_type=jnp.float32)
    totals = jnp.dot(selector.astype(jnp.float32), flat_wts, precision=lax.Precision.HIGHEST)
    sums = sums.reshape(blk_count, points, width)
    scaled = sums / jnp.maximum(totals, 1.0)[:, :, None]
    return scaled.reshape(blk_count * points, width).astype(jnp.bfloat16)


def solution(mesh):
    in_specs = (
        P(("groups", "view"), None, None),
        P(),
        P(("groups", "view"), None, None),
        P(("groups", "view"), None),
        P(("groups", "view"), None, None),
        P(("groups", "view"), None, None),
    )
    out_specs = P(("groups", "view"), None)
    return jax.shard_map(
        per_device, mesh=mesh, in_specs=in_specs, out_specs=out_specs, check_vma=False
    )
```

profile of v0, /device:TPU:12, one launch (start us, length us, event | category | flops | bytes accessed | tf_op | source)
XLA Modules:
  0.0 219.4 jit_solution(13881664905521372268)
XLA Ops:
  0.0 0.0 copy-start
  0.0 1.0 convert_reduce_fusion
  1.0 0.7 multiply_add_fusion.1
  1.6 0.8 select_reduce_fusion
  2.4 0.7 all_to_all.12
  3.1 6.3 %all-to-all-start = ((s32[16,1,16]{2,1,0:T(1,128)}), s32[16,1,16]{2,1,0:T(1,128)S(1)}, u32[]{:S(2)}, u32[]{:S(2)}) async-start(s32[16,1,16]{2,1,0:T(1,128)} %all_to_all.12), calls=%async_computation | async-start | bytes 16384 | tf_op jit(solution)/shard_map/all_to_all | solution.py:55
  9.4 1.0 fusion.20
  10.3 0.9 fusion.19
  11.3 0.0 copy-done
  11.3 7.0 %fusion.1 = f32[2048,768]{1,0:T(8,128)S(1)} fusion(f32[2048]{0:T(1024)S(1)} %bitcast.54, s32[2048]{0:T(1024)S(1)} %bitcast.60, f32[2048]{0:T(1024)S(1)} %bitcast.50, s32[2048]{0:T(1024)S(1)} %bitcast.62, f32[2048]{0:T(1024)S(1)} %bitcast.52, s32[2048]{0:T(1024)S(1)} %bitcast.58, f32[2048]{0:T(1024)S(1)} %bitcast.48, s32[2048]{0:T(1024)S(1)} %bitcast.56, ...), kind=kOutput, calls=%fused_computation.9 | convolution fusion | flops 3252682752 | bytes 7929856 | tf_op jit(solution)/shard_map/dot_general | solution.py:28
  18.3 0.0 copy-start.1
  18.3 9.0 %add_convert_fusion = bf16[2048,768]{1,0:T(8,128)(2,1)} fusion(f32[2048,768]{1,0:T(8,128)S(1)} %fusion.1, f32[2048]{0:T(1024)S(1)} %bitcast.55, s32[2048]{0:T(1024)S(1)} %bitcast.61, f32[2048]{0:T(1024)S(1)} %bitcast.51, s32[2048]{0:T(1024)S(1)} %bitcast.63, f32[2048]{0:T(1024)S(1)} %bitcast.53, s32[2048]{0:T(1024)S(1)} %bitcast.59, f32[2048]{0:T(1024)S(1)} %bitcast.49, ...), kind=kOutput, calls=%fused_computation.8 | convolution fusion | flops 3249537024 | bytes 11075584 | tf_op jit(solution)/shard_map/dot_general | solution.py:28
  27.3 0.0 copy-done.1
  27.4 0.1 reshape.82
  27.5 0.3 convolution_convert_fusion.2
  27.7 5.7 %reshape.79 = bf16[128,12288]{1,0:T(8,128)(2,1)} reshape(bf16[2048,768]{1,0:T(8,128)(2,1)} %add_convert_fusion) | data formatting | bytes 6291456 | tf_op jit(solution)/shard_map/reshape | solution.py:43
  33.5 0.7 reshape.96
  34.2 0.0 all-to-all-done
  34.2 6.0 %all-to-all-start.2 = ((bf16[16,2,128]{2,1,0:T(2,128)(2,1)}), bf16[16,2,128]{2,1,0:T(2,128)(2,1)S(1)}, u32[]{:S(2)}, u32[]{:S(2)}) async-start(bf16[16,2,128]{2,1,0:T(2,128)(2,1)} %reshape.96), calls=%async_computation.2 | async-start | bytes 16384 | tf_op jit(solution)/shard_map/all_to_all | solution.py:52
  40.2 3.7 %convolution_convert_fusion = bf16[256,12288]{1,0:T(8,128)(2,1)S(1)} fusion(bf16[128,12288]{1,0:T(8,128)(2,1)} %reshape.79, s32[128]{0:T(128)S(1)} %multiply_add_fusion.1), kind=kOutput, calls=%fused_computation | convolution fusion | flops 808484864 | bytes 9437696 | tf_op jit(solution)/shard_map/dot_general | solution.py:41
  43.9 4.5 %copy.17 = bf16[32,8,16,768]{3,2,1,0:T(8,128)(2,1)} copy(bf16[32,8,16,768]{3,1,2,0:T(8,128)(2,1)S(1)} %bitcast.43) | data formatting | bytes 12582912
  48.4 0.0 all-to-all-done.2
  48.4 0.0 copy-start.2
  48.4 6.2 %all-to-all-start.1 = ((bf16[16,16,16,768]{3,2,1,0:T(8,128)(2,1)}), bf16[16,16,16,768]{3,2,1,0:T(8,128)(2,1)}, u32[]{:S(2)}, u32[]{:S(2)}) async-start(bf16[16,16,16,768]{3,2,1,0:T(8,128)(2,1)} %bitcast.42), calls=%async_computation.1 | async-start | bytes 12582912 | tf_op jit(solution)/shard_map/all_to_all | solution.py:51
  54.5 0.5 broadcast.31
  55.1 0.7 reduce.4
  55.7 0.1 eq.125
  55.8 0.1 reshape.97
  55.9 0.2 convolution_maximum_fusion
  56.1 134.2 %all-to-all-done.1 = bf16[16,16,16,768]{3,2,1,0:T(8,128)(2,1)} async-done(((bf16[16,16,16,768]{3,2,1,0:T(8,128)(2,1)}), bf16[16,16,16,768]{3,2,1,0:T(8,128)(2,1)}, u32[]{:S(2)}, u32[]{:S(2)}) %all-to-all-start.1) | async-done | bytes 6291488 | tf_op jit(solution)/shard_map/all_to_all | solution.py:51
  190.3 0.0 copy-done.2
  190.3 8.2 %convolution_convert_fusion.1 = bf16[16,16,16,768]{3,2,1,0:T(8,128)(2,1)S(1)} fusion(bf16[16,16,16,768]{3,2,1,0:T(8,128)(2,1)} %all-to-all-done.1, bf16[768,768]{1,0:T(8,128)(2,1)S(1)} %copy-done.2), kind=kOutput, calls=%fused_computation.10 | convolution fusion | flops 4834983936 | bytes 13762560 | tf_op jit(solution)/shard_map/ncsd,de->ncse/dot_general | solution.py:56
  198.6 5.4 %copy.18 = bf16[32,8,16,768]{3,1,2,0:T(8,128)(2,1)} copy(bf16[32,8,16,768]{3,2,1,0:T(8,128)(2,1)S(1)} %bitcast.46) | data formatting | bytes 12582912
  204.0 8.6 %copy.11 = bf16[12288,256]{1,0:T(8,128)(2,1)} copy(bf16[12288,256]{0,1:T(8,128)(2,1)} %bitcast.44) | data formatting | bytes 12582912 | tf_op jit(solution)/shard_map/dot_general | solution.py:63
  212.6 4.8 %divide_convert_fusion = bf16[64,16,768]{2,0,1:T(8,128)(2,1)S(1)} fusion(bf16[16,768,256]{2,1,0:T(8,128)(2,1)} %bitcast.45, f32[64,16]{0,1:T(8,128)S(1)} %convolution_maximum_fusion, s32[256]{0:T(256)S(1)} %eq.125), kind=kOutput, calls=%fused_computation.11 | convolution fusion | flops 404242432 | bytes 7869440 | tf_op jit(solution)/shard_map/dot_general | solution.py:63
  217.4 2.0 copy.13
  (2 shorter events, 0.0 us)
Async XLA Ops:
  0.0 11.3 %copy-start = (bf16[1,1024,768]{2,1,0:T(8,128)(2,1)S(1)}, bf16[1,1024,768]{2,1,0:T(8,128)(2,1)}, u32[]{:S(2)}) copy-start(bf16[1,1024,768]{2,1,0:T(8,128)(2,1)} %param.6) | copy-start | bytes 4718596
  3.1 31.1 %all-to-all-start = ((s32[16,1,16]{2,1,0:T(1,128)}), s32[16,1,16]{2,1,0:T(1,128)S(1)}, u32[]{:S(2)}, u32[]{:S(2)}) async-start(s32[16,1,16]{2,1,0:T(1,128)} %all_to_all.12), calls=%async_computation | async-start | bytes 16384 | tf_op jit(solution)/shard_map/all_to_all | solution.py:55
  18.3 9.0 %copy-start.1 = (f32[1,4,2048]{2,1,0:T(4,128)S(1)}, f32[1,4,2048]{2,1,0:T(4,128)}, u32[]{:S(2)}) copy-start(f32[1,4,2048]{2,1,0:T(4,128)} %param.11) | copy-start | bytes 98308
  34.2 14.2 %all-to-all-start.2 = ((bf16[16,2,128]{2,1,0:T(2,128)(2,1)}), bf16[16,2,128]{2,1,0:T(2,128)(2,1)S(1)}, u32[]{:S(2)}, u32[]{:S(2)}) async-start(bf16[16,2,128]{2,1,0:T(2,128)(2,1)} %reshape.96), calls=%async_computation.2 | async-start | bytes 16384 | tf_op jit(solution)/shard_map/all_to_all | solution.py:52
  48.4 141.9 %copy-start.2 = (bf16[768,768]{1,0:T(8,128)(2,1)S(1)}, bf16[768,768]{1,0:T(8,128)(2,1)}, u32[]{:S(2)}) copy-start(bf16[768,768]{1,0:T(8,128)(2,1)} %param.7) | copy-start | bytes 3538948
  48.4 141.9 %all-to-all-start.1 = ((bf16[16,16,16,768]{3,2,1,0:T(8,128)(2,1)}), bf16[16,16,16,768]{3,2,1,0:T(8,128)(2,1)}, u32[]{:S(2)}, u32[]{:S(2)}) async-start(bf16[16,16,16,768]{3,2,1,0:T(8,128)(2,1)} %bitcast.42), calls=%async_computation.1 | async-start | bytes 12582912 | tf_op jit(solution)/shard_map/all_to_all | solution.py:51
where the time goes:
time: 222 us; the launch traced here: 219 us
  waiting for transfers between devices  134 us (60%)
  matrix products  33.2 us (15%)
  local copies, waits for them, and re-layouts  30.4 us (14%)
  starting transfers between devices  18.4 us (8%)
  other arithmetic  3.09 us (1%)
    all_to_all x1, waiting for transfers between devices, per_device(): lax.all_to_all(send_rows, 'view', split_axis=0, concat_axis=0, tiled=True)  134 us
    unnamed x10, local copies, waits for them, and re-layouts  10.8 us
    dot_general x1, matrix products, per_device(): jnp.dot(w_high, table, preferred_element_type=jnp.float32)  9.03 us
    dot_general x1, local copies, waits for them, and re-layouts, per_device(): jnp.dot(selector.astype(jnp.bfloat16), flat_rows, preferred_element_type=...  8.62 us
    dot_general x1, matrix products, per_device(): jnp.einsum('ncsd,de->ncse', rows_in, projection, preferred_element_type=j...  8.24 us
    dot_general x1, matrix products, per_device(): jnp.dot(w_low, table, preferred_element_type=jnp.float32)  7 us
    all_to_all x1, starting transfers between devices, per_device(): lax.all_to_all(send_ids, 'view', split_axis=0, concat_axis=0, tiled=True)  6.27 us
    all_to_all x1, starting transfers between devices, per_device(): lax.all_to_all(send_rows, 'view', split_axis=0, concat_axis=0, tiled=True)  6.15 us
  transfers between devices with their start and end apart: 3, of which 1 were waited for; matrix products, arithmetic and copies ran while one was open for 16% of the time, Pallas kernels for 0%

commit v1 on v0

--- a/solution.py
+++ b/solution.py
@@ -1,9 +1,309 @@
+import functools
+
 import jax
 import jax.numpy as jnp
 from jax import lax
+from jax.experimental import pallas as pl
+from jax.experimental.pallas import tpu as pltpu
 from jax.sharding import PartitionSpec as P
 
 BLK_DEV = 64
+KERNEL_VIEWS = 16
+CHUNK = 128
+META_ROWS = 16
+
+
+def flipped(index, bit):
+    return index + bit - 2 * bit * (lax.div(index, bit) % 2)
+
+
+def gather_sum_kernel(
+    emb_ref, proj_ref, meta_ref, out_ref,
+    table, sel, place, meta, compact, sums, landed, tots, landed_tots,
+    local_sem, meta_send, meta_recv, z_send, z_recv, x_send, x_recv,
+    core_send, core_recv, sum_send, sum_recv, tot_send, tot_recv,
+):
+    npatch = emb_ref.shape[0]
+    chunks = table.shape[0]
+    rows = meta_ref.shape[2]
+    points = place.shape[1]
+    group = lax.axis_index("groups")
+    me = lax.axis_index("view")
+    half = me // 8
+    z_peer, x_peer, core_peer = flipped(me, 4), flipped(me, 2), flipped(me, 1)
+    half_peers = []
+    for r in range(1, 8):
+        peer = me
+        for bit, axis in ((4, 1), (2, 2), (1, 4)):
+            if r & axis:
+                peer = flipped(peer, bit)
+        half_peers.append(peer)
+    across = (me + 8) % KERNEL_VIEWS
+    neighbours = half_peers + [across, flipped(across, 4)]
+    owner = [((me // 4) % 2) * 8 + e * 4 + me % 4 for e in range(2)]
+
+    def remote(src, dst, send_sem, recv_sem, peer):
+        return pltpu.make_async_remote_copy(
+            src_ref=src, dst_ref=dst, send_sem=send_sem, recv_sem=recv_sem,
+            device_id=(group, peer), device_id_type=pl.DeviceIdType.MESH,
+        )
+
+    def own_copy(c):
+        cols = pl.ds(pl.multiple_of(c * CHUNK, CHUNK), CHUNK)
+        return pltpu.make_async_copy(emb_ref.at[:, cols], table.at[c, 0], local_sem.at[c])
+
+    def z_copy(c):
+        return remote(table.at[c, 0], table.at[c, 1], z_send.at[c], z_recv.at[c], z_peer)
+
+    def x_copy(c, j):
+        return remote(table.at[c, j], table.at[c, 2 + j], x_send.at[c, j], x_recv.at[c, j], x_peer)
+
+    def core_copy(c, j):
+        return remote(
+            table.at[c, pl.ds(2 * j, 2)], table.at[c, pl.ds(4 + 2 * j, 2)],
+            core_send.at[c, j], core_recv.at[c, j], core_peer,
+        )
+
+    def meta_copy(r):
+        return remote(
+            meta_ref.at[half_peers[r - 1] % 8], meta.at[r], meta_send.at[r], meta_recv.at[r],
+            half_peers[r - 1],
+        )
+
+    def to_owner(src, dst, send_sem, recv_sem, e, start):
+        @pl.when(owner[e] == me)
+        def _():
+            if start:
+                pltpu.make_async_copy(src, dst, recv_sem).start()
+
+        @pl.when(owner[e] != me)
+        def _():
+            copy = remote(src, dst, send_sem, recv_sem, owner[e])
+            if start:
+                copy.start()
+            else:
+                copy.wait_send()
+
+    def sum_copy(c, e, start):
+        to_owner(
+            sums.at[c, e], landed.at[c, half], sum_send.at[c, e], sum_recv.at[c, half], e, start
+        )
+
+    def tot_copy(e, start):
+        to_owner(tots.at[e], landed_tots.at[half], tot_send.at[e], tot_recv.at[half], e, start)
+
+    own_meta = pltpu.make_async_copy(meta_ref.at[me % 8], meta.at[0], meta_recv.at[0])
+    own_meta.start()
+    for c in range(chunks):
+        own_copy(c).start()
+
+    barrier = pltpu.get_barrier_semaphore()
+    for peer in neighbours:
+        pl.semaphore_signal(
+            barrier, inc=1, device_id=(group, peer), device_id_type=pl.DeviceIdType.MESH
+        )
+    pl.semaphore_wait(barrier, len(neighbours))
+
+    for r in range(1, 8):
+        meta_copy(r).start()
+    for c in range(chunks):
+        own_copy(c).wait()
+        z_copy(c).start()
+        if c < 2:
+            x_copy(c, 0).start()
+
+    def forward_z(c):
+        z_copy(c).wait_recv()
+        x_copy(c, 1).start()
+        core_copy(c, 0).start()
+
+    def forward_x(c):
+        x_copy(c, 0).wait_recv()
+        x_copy(c, 1).wait_recv()
+        core_copy(c, 1).start()
+
+    own_meta.wait()
+    for r in range(1, 8):
+        meta_copy(r).wait_recv()
+    patch_ids = lax.broadcasted_iota(jnp.int32, (16, npatch), 1).astype(jnp.float32)
+
+    def build_sel(r):
+        @pl.loop(0, 2)
+        def _(e):
+            block = meta[r, pl.ds(pl.multiple_of(e * META_ROWS, META_ROWS), META_ROWS), :]
+            columns = jnp.concatenate(
+                [block, jnp.zeros((128 - META_ROWS, rows), jnp.float32)], axis=0
+            ).T
+            for i in range(rows // 16):
+                part = columns[16 * i : 16 * i + 16]
+                total = jnp.zeros((16, npatch), jnp.float32)
+                for k in range(4):
+                    total = total + jnp.where(
+                        part[:, k : k + 1] == patch_ids, part[:, 4 + k : 5 + k], 0.0
+                    )
+                sel[r, pl.ds(pl.multiple_of(e * rows + 16 * i, 16), 16), :] = total.astype(jnp.bfloat16)
+
+    def build_place(e):
+        for r in range(8):
+            dest = meta[r, e * META_ROWS + 8 : e * META_ROWS + 9, :]
+            step = 128
+
+            @pl.loop(0, points // step)
+            def _(i):
+                start = pl.multiple_of(i * step, step)
+                ids = lax.broadcasted_iota(jnp.int32, (step, rows), 0) + start
+                place[e, pl.ds(start, step), r * rows : (r + 1) * rows] = jnp.where(
+                    ids.astype(jnp.float32) == dest, 1.0, 0.0
+                ).astype(jnp.bfloat16)
+
+    forward_z(0)
+    pl.loop(0, 4)(build_sel)
+    forward_z(1)
+    forward_x(0)
+    pl.loop(4, 8)(build_sel)
+    build_place(0)
+    build_place(1)
+
+    row_ids = lax.broadcasted_iota(jnp.int32, (16, rows), 0)
+    for e in range(2):
+        total = jnp.zeros((16, points), jnp.float32)
+        for r in range(8):
+            wts = meta[r, e * META_ROWS + 4 : e * META_ROWS + 8, :]
+            wts = jnp.sum(wts, axis=0, keepdims=True)
+            high = wts.astype(jnp.bfloat16).astype(jnp.float32)
+            both = jnp.where(row_ids == 0, high, jnp.where(row_ids == 1, wts - high, 0.0))
+            total = total + lax.dot_general(
+                both.astype(jnp.bfloat16), place[e, :, r * rows : (r + 1) * rows],
+                (((1,), (1,)), ((), ())), preferred_element_type=jnp.float32,
+            )
+        tots[e] = jnp.broadcast_to(jnp.sum(total, axis=0, keepdims=True), (8, points))
+        tot_copy(e, True)
+
+    @pl.loop(0, chunks)
+    def _(c):
+        @pl.when(c + 2 < chunks)
+        def _():
+            x_copy(c + 2, 0).start()
+            forward_z(c + 2)
+
+        @pl.when(c + 1 < chunks)
+        def _():
+            forward_x(c + 1)
+
+        core_copy(c, 0).wait_recv()
+        core_copy(c, 1).wait_recv()
+
+        @pl.loop(0, 8)
+        def _(r):
+            blended = jnp.dot(sel[r], table[c, r], preferred_element_type=jnp.float32)
+            blended = blended.astype(jnp.bfloat16)
+            at = pl.ds(pl.multiple_of(r * rows, rows), rows)
+            compact[0, at, :] = blended[:rows]
+            compact[1, at, :] = blended[rows:]
+
+        for e in range(2):
+            sums[c, e] = jnp.dot(
+                place[e], compact[e], preferred_element_type=jnp.float32
+            ).astype(jnp.bfloat16)
+            sum_copy(c, e, True)
+
+    for h in range(2):
+        pltpu.make_async_copy(tots.at[0], landed_tots.at[h], tot_recv.at[h]).wait()
+    totals = landed_tots[0] + landed_tots[1]
+    totals = jnp.concatenate([totals, jnp.zeros((120, points), jnp.float32)], axis=0).T[:, 0:1]
+    parts = []
+    for c in range(chunks):
+        for h in range(2):
+            pltpu.make_async_copy(sums.at[c, 0], landed.at[c, h], sum_recv.at[c, h]).wait()
+        parts.append(
+            (landed[c, 0].astype(jnp.float32) + landed[c, 1].astype(jnp.float32)).astype(jnp.bfloat16)
+        )
+    whole = jnp.concatenate(parts, axis=1)
+    scaled = jnp.dot(whole, proj_ref[...], preferred_element_type=jnp.float32)
+    out_ref[...] = (scaled / jnp.maximum(totals, 1.0)).astype(out_ref.dtype)
+
+    for r in range(1, 8):
+        meta_copy(r).wait_send()
+    for e in range(2):
+        tot_copy(e, False)
+
+    @pl.loop(0, chunks)
+    def _(c):
+        z_copy(c).wait_send()
+        for j in range(2):
+            x_copy(c, j).wait_send()
+            core_copy(c, j).wait_send()
+            sum_copy(c, j, False)
+
+
+def pack_meta(owners, local_blocks, patches, weights):
+    slots = owners.shape[1]
+    points = patches.shape[2] // slots
+    cap = 2 * slots // KERNEL_VIEWS
+    target = owners[0, :, 0]
+    slot_ids = jnp.arange(slots, dtype=jnp.int32)
+    earlier = slot_ids[None, :] < slot_ids[:, None]
+    rank = jnp.sum(((target[:, None] == target[None, :]) & earlier).astype(jnp.int32), axis=1)
+    handler = (target // 8) * 4 + target % 4
+    position = (handler * 2 + (target // 4) % 2) * cap + rank
+    placing = jnp.arange(KERNEL_VIEWS * cap, dtype=jnp.int32)[:, None] == position[None, :]
+    dest = local_blocks[0][:, None] * points + jnp.arange(points, dtype=jnp.int32)[None, :] + 1
+    values = jnp.concatenate(
+        [
+            patches[0].reshape(4, slots, points).astype(jnp.float32),
+            weights[0].reshape(4, slots, points),
+            dest[None].astype(jnp.float32),
+        ],
+        axis=0,
+    )
+    packed = jnp.einsum(
+        "ksj,ps->kpj", values, placing.astype(jnp.float32), precision=lax.Precision.HIGHEST
+    )
+    packed = packed.reshape(9, KERNEL_VIEWS, cap * points)
+    packed = jnp.concatenate(
+        [packed[:8], packed[8:] - 1.0, jnp.zeros((META_ROWS - 9,) + packed.shape[1:], jnp.float32)],
+        axis=0,
+    )
+    return packed.transpose(1, 0, 2).reshape(8, 2 * META_ROWS, cap * points)
+
+
+def per_device_kernel(embeddings, projection, owners, local_blocks, patches, weights):
+    npatch, width = embeddings.shape[1:]
+    slots = owners.shape[1]
+    points = BLK_DEV * patches.shape[2] // slots
+    chunks = width // CHUNK
+    meta = pack_meta(owners, local_blocks, patches, weights)
+    rows = meta.shape[2]
+    bf16, f32 = jnp.bfloat16, jnp.float32
+    dma = pltpu.SemaphoreType.DMA
+    vmem = pl.BlockSpec(memory_space=pltpu.VMEM)
+    return pl.pallas_call(
+        gather_sum_kernel,
+        out_shape=jax.ShapeDtypeStruct((points, width), bf16),
+        in_specs=[pl.BlockSpec(memory_space=pl.ANY), vmem, vmem],
+        out_specs=vmem,
+        scratch_shapes=[
+            pltpu.VMEM((chunks, 8, npatch, CHUNK), bf16),
+            pltpu.VMEM((8, 2 * rows, npatch), bf16),
+            pltpu.VMEM((2, points, 8 * rows), bf16),
+            pltpu.VMEM((8, 2 * META_ROWS, rows), f32),
+            pltpu.VMEM((2, 8 * rows, CHUNK), bf16),
+            pltpu.VMEM((chunks, 2, points, CHUNK), bf16),
+            pltpu.VMEM((chunks, 2, points, CHUNK), bf16),
+            pltpu.VMEM((2, 8, points), f32),
+            pltpu.VMEM((2, 8, points), f32),
+            dma((chunks,)),
+            dma((8,)), dma((8,)),
+            dma((chunks,)), dma((chunks,)),
+            dma((chunks, 2)), dma((chunks, 2)),
+            dma((chunks, 2)), dma((chunks, 2)),
+            dma((chunks, 2)), dma((chunks, 2)),
+            dma((2,)), dma((2,)),
+        ],
+        compiler_params=pltpu.CompilerParams(
+            collective_id=0, has_side_effects=True, vmem_limit_bytes=60 * 1024 * 1024
+        ),
+    )(embeddings[0], projection, meta)
 
 
 def per_device(embeddings, projection, owners, local_blocks, patches, weights):
@@ -77,6 +377,7 @@
         P(("groups", "view"), None, None),
     )
     out_specs = P(("groups", "view"), None)
+    body = per_device_kernel if mesh.shape["view"] == KERNEL_VIEWS else per_device
     return jax.shard_map(
-        per_device, mesh=mesh, in_specs=in_specs, out_specs=out_specs, check_vma=False
-    )
+        body, mesh=mesh, in_specs=in_specs, out_specs=out_specs, check_vma=False
+    )

time: 222 us -> 124 us (0.56); the launches traced: 219 us -> 124 us
  waiting for transfers between devices: 134 us -> 0 us
  Pallas kernels: 0 us -> 115 us
  matrix products: 33.2 us -> 0.24 us
  local copies, waits for them, and re-layouts: 30.4 us -> 5.79 us
  starting transfers between devices: 18.4 us -> 0 us
    all_to_all x3 -> x0, waiting for transfers between devices: 134 us -> none  [the longest x1 134 us: per_device(): lax.all_to_all(send_rows, 'view', split_axis=0, concat_axis=0, tiled=True)]
    pallas_call x0 -> x1, Pallas kernels: none -> 115 us  [per_device_kernel(): pl.pallas_call(gather_sum_kernel, out_shape=jax.ShapeDtypeStruct((points,...]
    dot_general x7 -> x0, matrix products: 33.2 us -> none  [the longest x1 9.03 us: per_device(): jnp.dot(w_high, table, preferred_element_type=jnp.float32)]
    all_to_all x3 -> x0, starting transfers between devices: 18.4 us -> none  [the longest x1 6.27 us: per_device(): lax.all_to_all(send_ids, 'view', split_axis=0, concat_axis=0, tiled=True)]
    dot_general x1 -> x0, local copies, waits for them, and re-layouts: 8.62 us -> none  [per_device(): jnp.dot(selector.astype(jnp.bfloat16), flat_rows, preferred_element_type=...]
    unnamed x10 -> x1, local copies, waits for them, and re-layouts: 10.8 us -> 2.65 us
    reshape x2 -> x0, local copies, waits for them, and re-layouts: 5.81 us -> none  [the longest x1 5.73 us: per_device(): blended.reshape(slots, points * width)]
  transfers between devices with their start and end apart: 3 -> 0, of which waited for: 1 -> 0; matrix products, arithmetic and copies ran while one was open for 16% -> 0% of each run, Pallas kernels for 0% -> 0%
where the time goes in v1:
time: 124 us
  Pallas kernels  115 us (93%)
  local copies, waits for them, and re-layouts  5.79 us (5%)
  other arithmetic  3.1 us (2%)
    pallas_call x1, Pallas kernels, per_device_kernel(): pl.pallas_call(gather_sum_kernel, out_shape=jax.ShapeDtypeStruct((points,...  115 us
    unnamed x1, local copies, waits for them, and re-layouts  2.65 us

profile of v1, /device:TPU:12, one launch (start us, length us, event | category | flops | bytes accessed | tf_op | source)
XLA Modules:
  0.0 124.2 jit_solution(3500579124302865771)
XLA Ops:
  0.0 0.7 multiply_bitcast_fusion
  0.7 0.9 convert_reduce_fusion
  1.6 0.7 multiply_add_fusion
  2.3 0.1 pad.2.clone
  2.3 0.8 convert_element_type.22
  3.1 0.1 convert_element_type.23
  3.2 0.1 copy.12
  3.3 0.9 reshape_squeeze.4
  4.2 0.1 copy.13
  4.3 0.2 fusion
  4.6 0.1 copy.15
  4.7 0.1 sub.19
  4.8 0.3 copy.14
  5.2 0.4 slice.11
  5.6 0.1 maximum_bitcast_fusion
  5.7 0.9 copy.16
  6.6 114.9 %shard_map.64 = bf16[1024,768]{1,0:T(8,128)(2,1)} custom-call(bf16[1024,768]{1,0:T(8,128)(2,1)} %bitcast.15, bf16[768,768]{1,0:T(8,128)(2,1)} %proj_ref.1, f32[8,32,256]{2,1,0:T(8,128)} %bitcast.16), custom_call_target="tpu_custom_call" | custom-call | tf_op jit(solution)/shard_map/pallas_call | solution.py:280
  121.5 2.7 %copy.18 = bf16[1024,768]{1,0:T(8,128)(2,1)} copy(bf16[1024,768]{1,0:T(8,128)(2,1)} %shard_map.64) | data formatting | bytes 3145728
  (5 shorter events, 0.0 us)

commit v2 on v1

--- a/solution.py
+++ b/solution.py
@@ -19,7 +19,7 @@
 
 def gather_sum_kernel(
     emb_ref, proj_ref, meta_ref, out_ref,
-    table, sel, place, meta, compact, sums, landed, tots, landed_tots,
+    table, sel, place, meta, wcols, compact, sums, landed, total, tots, landed_tots,
     local_sem, meta_send, meta_recv, z_send, z_recv, x_send, x_recv,
     core_send, core_recv, sum_send, sum_recv, tot_send, tot_recv,
 ):
@@ -108,8 +108,9 @@
         meta_copy(r).start()
     for c in range(chunks):
         own_copy(c).wait()
-        z_copy(c).start()
-        if c < 2:
+        if c < 3:
+            z_copy(c).start()
+        if c == 0:
             x_copy(c, 0).start()
 
     def forward_z(c):
@@ -142,6 +143,11 @@
                         part[:, k : k + 1] == patch_ids, part[:, 4 + k : 5 + k], 0.0
                     )
                 sel[r, pl.ds(pl.multiple_of(e * rows + 16 * i, 16), 16), :] = total.astype(jnp.bfloat16)
+            wts = jnp.sum(columns[:, 4:8], axis=1, keepdims=True)
+            high = wts.astype(jnp.bfloat16).astype(jnp.float32)
+            lanes = lax.broadcasted_iota(jnp.int32, (rows, CHUNK), 1)
+            both = jnp.where(lanes == 0, high, jnp.where(lanes == 1, wts - high, 0.0))
+            wcols[e, pl.ds(pl.multiple_of(r * rows, rows), rows), :] = both.astype(jnp.bfloat16)
 
     def build_place(e):
         for r in range(8):
@@ -156,44 +162,39 @@
                     ids.astype(jnp.float32) == dest, 1.0, 0.0
                 ).astype(jnp.bfloat16)
 
+    def project(c):
+        for h in range(2):
+            pltpu.make_async_copy(sums.at[c, 0], landed.at[c, h], sum_recv.at[c, h]).wait()
+        chunk = (landed[c, 0].astype(jnp.float32) + landed[c, 1].astype(jnp.float32)).astype(
+            jnp.bfloat16
+        )
+        at = pl.ds(pl.multiple_of(c * CHUNK, CHUNK), CHUNK)
+        return jnp.dot(chunk, proj_ref[at, :], preferred_element_type=jnp.float32)
+
+    pl.loop(0, 3)(build_sel)
     forward_z(0)
-    pl.loop(0, 4)(build_sel)
+    x_copy(1, 0).start()
+    pl.loop(3, 8)(build_sel)
     forward_z(1)
-    forward_x(0)
-    pl.loop(4, 8)(build_sel)
     build_place(0)
     build_place(1)
-
-    row_ids = lax.broadcasted_iota(jnp.int32, (16, rows), 0)
-    for e in range(2):
-        total = jnp.zeros((16, points), jnp.float32)
-        for r in range(8):
-            wts = meta[r, e * META_ROWS + 4 : e * META_ROWS + 8, :]
-            wts = jnp.sum(wts, axis=0, keepdims=True)
-            high = wts.astype(jnp.bfloat16).astype(jnp.float32)
-            both = jnp.where(row_ids == 0, high, jnp.where(row_ids == 1, wts - high, 0.0))
-            total = total + lax.dot_general(
-                both.astype(jnp.bfloat16), place[e, :, r * rows : (r + 1) * rows],
-                (((1,), (1,)), ((), ())), preferred_element_type=jnp.float32,
-            )
-        tots[e] = jnp.broadcast_to(jnp.sum(total, axis=0, keepdims=True), (8, points))
-        tot_copy(e, True)
+    forward_x(0)
 
     @pl.loop(0, chunks)
     def _(c):
+        @pl.when(c + 3 < chunks)
+        def _():
+            z_copy(c + 3).start()
+
         @pl.when(c + 2 < chunks)
         def _():
             x_copy(c + 2, 0).start()
             forward_z(c + 2)
 
-        @pl.when(c + 1 < chunks)
-        def _():
-            forward_x(c + 1)
-
         core_copy(c, 0).wait_recv()
         core_copy(c, 1).wait_recv()
 
-        @pl.loop(0, 8)
+        @pl.loop(0, 8, unroll=4)
         def _(r):
             blended = jnp.dot(sel[r], table[c, r], preferred_element_type=jnp.float32)
             blended = blended.astype(jnp.bfloat16)
@@ -207,20 +208,32 @@
             ).astype(jnp.bfloat16)
             sum_copy(c, e, True)
 
+        @pl.when(c == 0)
+        def _():
+            for e in range(2):
+                both = jnp.dot(place[e], wcols[e], preferred_element_type=jnp.float32).T
+                tots[e] = jnp.broadcast_to(both[0:1] + both[1:2], (8, points))
+                tot_copy(e, True)
+
+        @pl.when(c + 1 < chunks)
+        def _():
+            forward_x(c + 1)
+
+        @pl.when(c == 2)
+        def _():
+            total[...] = project(0)
+
+        @pl.when(c > 2)
+        def _():
+            total[...] += project(c - 2)
+
     for h in range(2):
         pltpu.make_async_copy(tots.at[0], landed_tots.at[h], tot_recv.at[h]).wait()
     totals = landed_tots[0] + landed_tots[1]
     totals = jnp.concatenate([totals, jnp.zeros((120, points), jnp.float32)], axis=0).T[:, 0:1]
-    parts = []
-    for c in range(chunks):
-        for h in range(2):
-            pltpu.make_async_copy(sums.at[c, 0], landed.at[c, h], sum_recv.at[c, h]).wait()
-        parts.append(
-            (landed[c, 0].astype(jnp.float32) + landed[c, 1].astype(jnp.float32)).astype(jnp.bfloat16)
-        )
-    whole = jnp.concatenate(parts, axis=1)
-    scaled = jnp.dot(whole, proj_ref[...], preferred_element_type=jnp.float32)
-    out_ref[...] = (scaled / jnp.maximum(totals, 1.0)).astype(out_ref.dtype)
+    inverse = 1.0 / jnp.maximum(totals, 1.0)
+    total[...] += project(chunks - 2)
+    out_ref[...] = ((total[...] + project(chunks - 1)) * inverse).astype(out_ref.dtype)
 
     for r in range(1, 8):
         meta_copy(r).wait_send()
@@ -288,8 +301,10 @@
             pltpu.VMEM((2, points, 8 * rows), bf16),
             pltpu.VMEM((8, 2 * META_ROWS, rows), f32),
             pltpu.VMEM((2, 8 * rows, CHUNK), bf16),
+            pltpu.VMEM((2, 8 * rows, CHUNK), bf16),
             pltpu.VMEM((chunks, 2, points, CHUNK), bf16),
             pltpu.VMEM((chunks, 2, points, CHUNK), bf16),
+            pltpu.VMEM((points, width), f32),
             pltpu.VMEM((2, 8, points), f32),
             pltpu.VMEM((2, 8, points), f32),
             dma((chunks,)),

time: 124 us -> 115 us (0.927)
  Pallas kernels: 115 us -> 105 us
    pallas_call x1, Pallas kernels: 115 us -> 105 us  [per_device_kernel(): pl.pallas_call(gather_sum_kernel, out_shape=jax.ShapeDtypeStruct((points,...]
where the time goes in v2:
time: 115 us
  Pallas kernels  105 us (91%)
  local copies, waits for them, and re-layouts  5.79 us (5%)
  other arithmetic  3.1 us (3%)
    pallas_call x1, Pallas kernels, per_device_kernel(): pl.pallas_call(gather_sum_kernel, out_shape=jax.ShapeDtypeStruct((points,...  105 us
    unnamed x1, local copies, waits for them, and re-layouts  2.65 us

profile of v2, /device:TPU:12, one launch (start us, length us, event | category | flops | bytes accessed | tf_op | source)
XLA Modules:
  0.0 114.5 jit_solution(6657224725595160364)
XLA Ops:
  0.0 0.7 multiply_bitcast_fusion
  0.7 0.9 convert_reduce_fusion
  1.6 0.7 multiply_add_fusion
  2.3 0.1 pad.2.clone
  2.3 0.8 convert_element_type.22
  3.1 0.1 convert_element_type.23
  3.2 0.1 copy.12
  3.3 0.9 reshape_squeeze.4
  4.2 0.1 copy.13
  4.3 0.2 fusion
  4.6 0.1 copy.15
  4.7 0.1 sub.19
  4.8 0.3 copy.14
  5.2 0.4 slice.11
  5.6 0.1 maximum_bitcast_fusion
  5.7 0.9 copy.16
  6.6 105.3 %shard_map.64 = bf16[1024,768]{1,0:T(8,128)(2,1)} custom-call(bf16[1024,768]{1,0:T(8,128)(2,1)} %bitcast.15, bf16[768,768]{1,0:T(8,128)(2,1)} %proj_ref.1, f32[8,32,256]{2,1,0:T(8,128)} %bitcast.16), custom_call_target="tpu_custom_call" | custom-call | tf_op jit(solution)/shard_map/pallas_call | solution.py:293
  111.9 2.7 %copy.18 = bf16[1024,768]{1,0:T(8,128)(2,1)} copy(bf16[1024,768]{1,0:T(8,128)(2,1)} %shard_map.64) | data formatting | bytes 3145728
  (5 shorter events, 0.0 us)

commit v3 on v2

--- a/solution.py
+++ b/solution.py
@@ -165,12 +165,16 @@
     def project(c):
         for h in range(2):
             pltpu.make_async_copy(sums.at[c, 0], landed.at[c, h], sum_recv.at[c, h]).wait()
-        chunk = (landed[c, 0].astype(jnp.float32) + landed[c, 1].astype(jnp.float32)).astype(
-            jnp.bfloat16
-        )
-        at = pl.ds(pl.multiple_of(c * CHUNK, CHUNK), CHUNK)
-        return jnp.dot(chunk, proj_ref[at, :], preferred_element_type=jnp.float32)
-
+        cols = pl.ds(pl.multiple_of(c * CHUNK, CHUNK), CHUNK)
+
+        @pl.loop(0, points // rows)
+        def _(i):
+            at = pl.ds(pl.multiple_of(i * rows, rows), rows)
+            near = landed[c, 0, at, :].astype(jnp.float32)
+            chunk = (near + landed[c, 1, at, :].astype(jnp.float32)).astype(jnp.bfloat16)
+            total[at, :] += jnp.dot(chunk, proj_ref[cols, :], preferred_element_type=jnp.float32)
+
+    total[...] = jnp.zeros_like(total)
     pl.loop(0, 3)(build_sel)
     forward_z(0)
     x_copy(1, 0).start()
@@ -194,15 +198,15 @@
         core_copy(c, 0).wait_recv()
         core_copy(c, 1).wait_recv()
 
-        @pl.loop(0, 8, unroll=4)
-        def _(r):
-            blended = jnp.dot(sel[r], table[c, r], preferred_element_type=jnp.float32)
-            blended = blended.astype(jnp.bfloat16)
-            at = pl.ds(pl.multiple_of(r * rows, rows), rows)
-            compact[0, at, :] = blended[:rows]
-            compact[1, at, :] = blended[rows:]
-
         for e in range(2):
+            @pl.loop(0, 8)
+            def _(r):
+                blended = jnp.dot(
+                    sel[r, e * rows : (e + 1) * rows], table[c, r], preferred_element_type=jnp.float32
+                )
+                at = pl.ds(pl.multiple_of(r * rows, rows), rows)
+                compact[e, at, :] = blended.astype(jnp.bfloat16)
+
             sums[c, e] = jnp.dot(
                 place[e], compact[e], preferred_element_type=jnp.float32
             ).astype(jnp.bfloat16)
@@ -219,21 +223,17 @@
         def _():
             forward_x(c + 1)
 
-        @pl.when(c == 2)
-        def _():
-            total[...] = project(0)
-
-        @pl.when(c > 2)
-        def _():
-            total[...] += project(c - 2)
+        @pl.when(c >= 2)
+        def _():
+            project(c - 2)
 
     for h in range(2):
         pltpu.make_async_copy(tots.at[0], landed_tots.at[h], tot_recv.at[h]).wait()
     totals = landed_tots[0] + landed_tots[1]
     totals = jnp.concatenate([totals, jnp.zeros((120, points), jnp.float32)], axis=0).T[:, 0:1]
     inverse = 1.0 / jnp.maximum(totals, 1.0)
-    total[...] += project(chunks - 2)
-    out_ref[...] = ((total[...] + project(chunks - 1)) * inverse).astype(out_ref.dtype)
+    pl.loop(chunks - 2, chunks)(project)
+    out_ref[...] = (total[...] * inverse).astype(out_ref.dtype)
 
     for r in range(1, 8):
         meta_copy(r).wait_send()

time: 115 us -> 115 us (level)
  no operation moved by 1% of the time
where the time goes in v3:
time: 115 us; the launch traced here: 114 us
  Pallas kernels  104 us (90%)
  local copies, waits for them, and re-layouts  5.79 us (5%)
  other arithmetic  3.1 us (3%)
    pallas_call x1, Pallas kernels, per_device_kernel(): pl.pallas_call(gather_sum_kernel, out_shape=jax.ShapeDtypeStruct((points,...  104 us
    unnamed x1, local copies, waits for them, and re-layouts  2.65 us

profile of v3, /device:TPU:12, one launch (start us, length us, event | category | flops | bytes accessed | tf_op | source)
XLA Modules:
  0.0 113.7 jit_solution(881342495274325274)
XLA Ops:
  0.0 0.7 multiply_bitcast_fusion
  0.7 0.9 convert_reduce_fusion
  1.6 0.7 multiply_add_fusion
  2.3 0.1 pad.2.clone
  2.3 0.8 convert_element_type.22
  3.1 0.1 convert_element_type.23
  3.2 0.1 copy.12
  3.3 0.9 reshape_squeeze.4
  4.2 0.1 copy.13
  4.3 0.2 fusion
  4.6 0.1 copy.15
  4.7 0.1 sub.19
  4.8 0.3 copy.14
  5.2 0.4 slice.11
  5.6 0.1 maximum_bitcast_fusion
  5.7 0.9 copy.16
  6.6 104.5 %shard_map.64 = bf16[1024,768]{1,0:T(8,128)(2,1)} custom-call(bf16[1024,768]{1,0:T(8,128)(2,1)} %bitcast.15, bf16[768,768]{1,0:T(8,128)(2,1)} %proj_ref.1, f32[8,32,256]{2,1,0:T(8,128)} %bitcast.16), custom_call_target="tpu_custom_call" | custom-call | tf_op jit(solution)/shard_map/pallas_call | solution.py:293
  111.1 2.7 %copy.18 = bf16[1024,768]{1,0:T(8,128)(2,1)} copy(bf16[1024,768]{1,0:T(8,128)(2,1)} %shard_map.64) | data formatting | bytes 3145728
  (5 shorter events, 0.0 us)
